TPU v7x, 32 devices: a whole 2x2x4 slice. The times are simulated.
32 devices in a mesh: row: 8 (over z, core), col: 4 (over y, x).
Axes of the slice: x: 2, y: 2, z: 4, core: 2. Of those that a mesh axis runs over, the one named last changes fastest.
Arguments:
- pair: bfloat16 [128, 128, 128], P('row', 'col'), may hold values from -6 to 6
- pair_mask: int32 [128, 128], P('row', 'col'), may hold values 0 or 1
- in_weights: bfloat16 [128, 512], replicated, may hold values from -0.5 to 0.5
- gate_weight: bfloat16 [128, 128], replicated, may hold values from -0.5 to 0.5
- out_weight: bfloat16 [128, 128], replicated, may hold values from -0.5 to 0.5
Outputs:
- update: bfloat16 [128, 128, 128], P('row', 'col')
All inputs are finite; a program needn't handle non-finite values. No bound on the sum of `pair_mask` on one device may be relied on, other than what follows from the above.
Results may differ from a plain program's by a relative error of at most 0.0078.
Values may be sent and summed in bfloat16 or wider, within the bound.
No kernel may reach another device: no remote copies, remote signals or barrier semaphores. Data moves between devices by JAX's collectives and lax.ppermute only.
A program may use at most 64 MiB of HBM per device.

v0:
```python
import jax
import jax.numpy as jnp
from jax import lax
from jax.sharding import PartitionSpec as P


def spread(value, axis, root):
    mine = lax.axis_index(axis) == root
    return lax.psum(jnp.where(mine, value, jnp.zeros_like(value)), axis)


def layer_norm(values):
    mean = jnp.mean(values, axis=-1, keepdims=True)
    centred = values - mean
    var = jnp.mean(centred * centred, axis=-1, keepdims=True)
    return centred * jax.lax.rsqrt(var + 1e-05)


def body(pair, pair_mask, in_weights, gate_weight, out_weight):
    rows_here = pair.shape[0]
    cols_here = pair.shape[1]
    width = pair.shape[2]
    hidden = in_weights.shape[1] // 4
    normed = layer_norm(pair.reshape(-1, width).astype(jnp.float32)).astype(jnp.bfloat16)
    proj = jnp.dot(normed, in_weights, preferred_element_type=jnp.float32)
    maskf = pair_mask.reshape(-1, 1).astype(jnp.float32)
    left = (maskf * jax.nn.sigmoid(proj[:, hidden : 2 * hidden]) * proj[:, :hidden]).astype(
        jnp.bfloat16
    )
    right = (
        maskf * jax.nn.sigmoid(proj[:, 3 * hidden :]) * proj[:, 2 * hidden : 3 * hidden]
    ).astype(jnp.bfloat16)
    left = left.reshape(rows_here, cols_here, hidden)
    right = right.reshape(rows_here, cols_here, hidden)
    gate = jax.nn.sigmoid(jnp.dot(normed, gate_weight, preferred_element_type=jnp.float32))
    ratio = lax.axis_size("row") // lax.axis_size("col")
    column = lax.axis_index("col")
    left_rows, right_rows = (
        lax.all_gather(left, "col", axis=1, tiled=True),
        lax.all_gather(right, "col", axis=1, tiled=True),
    )
    blocks = [spread(right_rows, "row", ratio * column + offset) for offset in range(ratio)]
    partner = jnp.concatenate(blocks, axis=0)
    tri = jnp.einsum("ikc,jkc->ijc", left_rows, partner, preferred_element_type=jnp.float32)
    tnorm = layer_norm(tri.reshape(-1, hidden)).astype(jnp.bfloat16)
    update = gate * jnp.dot(tnorm, out_weight, preferred_element_type=jnp.float32)
    return update.astype(jnp.bfloat16).reshape(rows_here, cols_here, width)


def solution(mesh):
    in_specs = (P("row", "col", None), P("row", "col"), P(), P(), P())
    out_specs = P("row", "col", None)
    return jax.shard_map(body, mesh=mesh, in_specs=in_specs, out_specs=out_specs, check_vma=False)
```

profile of v0, /device:TPU:0, one launch (start us, length us, event | category | flops | bytes accessed | tf_op | source)
XLA Modules:
  0.0 95.0 jit_solution(5140240427640854854)
XLA Ops:
  6.5 1.1 %convert_reduce_fusion = f32[16,32]{1,0:T(8,128)S(1)} fusion(bf16[16,32,128]{2,1,0:T(8,128)(2,1)} %param.5), kind=kLoop, calls=%fused_computation.34 | loop fusion | flops 130560 | bytes 133120 | tf_op jit(solution)/shard_map/reduce_sum | solution.py:13
  7.6 1.2 %multiply_reduce_fusion.1 = f32[16,32]{1,0:T(8,128)S(1)} fusion(bf16[16,32,128]{2,1,0:T(8,128)(2,1)} %param.5, f32[16,32]{1,0:T(8,128)S(1)} %broadcast_multiply_fusion.1), kind=kLoop, calls=%fused_computation.33 | loop fusion | flops 261632 | bytes 135168 | tf_op jit(solution)/shard_map/reduce_sum | solution.py:15
  8.8 0.1 div.26
  8.9 0.1 rsqrt.23
  9.0 0.7 convert_element_type.40
  9.7 0.1 convert_element_type.41
  9.8 1.1 %fusion.20 = bf16[512,128]{1,0:T(8,128)(2,1)S(1)} fusion(bf16[16,32,128]{2,1,0:T(8,128)(2,1)} %param.5, f32[512]{0:T(512)S(1)} %rsqrt.23, f32[512]{0:T(512)S(1)} %div.26), kind=kLoop, calls=%fused_computation.32 | loop fusion | flops 262144 | bytes 266240 | tf_op jit(solution)/shard_map/convert_element_type | solution.py:24
  10.9 0.3 fusion.23
  11.1 0.2 fusion.12
  11.4 11.5 %all_gather.6 = bf16[16,128,128]{2,0,1:T(8,128)(2,1)S(1)} all-gather(bf16[16,32,128]{2,0,1:T(8,128)(2,1)S(1)} %copy.11), channel_id=1, replica_groups=mesh['row'=8,'col'=4] {'col'}, dimensions={1}, use_global_device_ids=true | all-gather | bytes 655360 | tf_op jit(solution)/shard_map/all_gather | solution.py:40
  22.9 0.7 copy.12
  23.6 1.1 %broadcast_select_fusion.1 = (bf16[16,128,128]{1,0,2:T(8,128)(2,1)}, bf16[16,128,128]{1,0,2:T(8,128)(2,1)}) fusion(bf16[16,128,128]{1,0,2:T(8,128)(2,1)S(1)} %copy.12, pred[]{:T(512)S(6)} %eq.6, pred[]{:T(512)S(6)} %eq.7), kind=kLoop, calls=%fused_computation.12 | loop fusion | flops 524288 | bytes 1572866 | tf_op jit(solution)/shard_map/jit(_where)/select_n | solution.py:9
  24.9 10.2 %all_gather.7 = bf16[16,128,128]{2,0,1:T(8,128)(2,1)S(1)} all-gather(bf16[16,32,128]{2,0,1:T(8,128)(2,1)S(1)} %copy.14), channel_id=1, replica_groups=mesh['row'=8,'col'=4] {'col'}, dimensions={1}, use_global_device_ids=true | all-gather | bytes 655360 | tf_op jit(solution)/shard_map/all_gather | solution.py:39
  35.0 0.7 copy.15
  35.8 0.2 fusion.2
  36.0 48.2 %all-reduce.3.cloned.1.call-done = (bf16[16,128,128]{1,0,2:T(8,128)(2,1)}, bf16[16,128,128]{1,0,2:T(8,128)(2,1)}) async-done(((bf16[16,128,128]{1,0,2:T(8,128)(2,1)}, bf16[16,128,128]{1,0,2:T(8,128)(2,1)}), (bf16[16,128,128]{1,0,2:T(8,128)(2,1)}, bf16[16,128,128]{1,0,2:T(8,128)(2,1)})) %all-reduce.3.cloned.1.call-update) | async-done | bytes 1048592 | tf_op jit(solution)/shard_map/psum | solution.py:9
  84.2 1.9 %fusion.22 = (f32[16,32]{1,0:T(8,128)S(1)}, f32[16,32,128]{1,0,2:T(8,128)S(1)}) fusion(bf16[16,128,128]{1,0,2:T(8,128)(2,1)S(1)} %copy.15, bf16[16,128,128]{1,0,2:T(8,128)(2,1)} %get-tuple-element.5, bf16[16,128,128]{1,0,2:T(8,128)(2,1)} %get-tuple-element.6), kind=kOutput, calls=%fused_computation.40 | convolution fusion | flops 18939392 | bytes 1837056 | tf_op jit(solution)/shard_map/ikc,jkc->ijc/dot_general | solution.py:44
  86.1 0.4 copy.16
  86.5 0.2 multiply_reduce_fusion
  86.7 0.1 div.32
  86.8 0.1 rsqrt.25
  86.9 0.2 fusion.18
  87.1 0.2 copy-done.1
  87.3 0.8 fusion.3
  (13 shorter events, 0.2 us)
Async XLA Ops:
  6.5 4.3 %copy-start = (bf16[128,512]{1,0:T(8,128)(2,1)S(1)}, bf16[128,512]{1,0:T(8,128)(2,1)}, u32[]{:S(2)}) copy-start(bf16[128,512]{1,0:T(8,128)(2,1)} %param.7) | copy-start | bytes 393220
  6.5 77.7 %all-reduce.3.cloned.1.call-start = ((), (), s32[]{:S(2)}) async-start(), calls=%async_computation | async-start | bytes 2097152 | tf_op jit(solution)/shard_map/psum | solution.py:9
  24.8 11.0 %copy-start.2 = (bf16[128,128]{1,0:T(8,128)(2,1)S(1)}, bf16[128,128]{1,0:T(8,128)(2,1)}, u32[]{:S(2)}) copy-start(bf16[128,128]{1,0:T(8,128)(2,1)} %param.8) | copy-start | bytes 98308
  86.5 0.8 copy-start.1
Sparse Core Ops, SparseCore 0:
  24.9 59.2 all-reduce.2
where the time goes:
time: 95.3 us; the launch traced here: 95 us
  waiting for transfers between devices  48.3 us (51%)
  blocking collectives  21.7 us (23%)
  between operations  13.5 us (14%)
  other arithmetic  5.74 us (6%)
  matrix products  3.17 us (3%)
  local copies, waits for them, and re-layouts  2.59 us (3%)
    psum x1, waiting for transfers between devices, spread(): return lax.psum(jnp.where(mine, value, jnp.zeros_like(value)), axis)  48.2 us
    all_gather x1, blocking collectives, body(): lax.all_gather(right, 'col', axis=1, tiled=True)  11.5 us
    all_gather x1, blocking collectives, body(): lax.all_gather(left, 'col', axis=1, tiled=True)  10.2 us
  transfers between devices with their start and end apart: 1, of which 1 were waited for; matrix products, arithmetic and copies ran while one was open for 1% of the time, Pallas kernels for 0%

commit v1 on v0

--- a/solution.py
+++ b/solution.py
@@ -1,7 +1,14 @@
+import functools
+import math
+
 import jax
 import jax.numpy as jnp
 from jax import lax
+from jax.experimental import pallas as pl
+from jax.experimental.pallas import tpu as pltpu
 from jax.sharding import PartitionSpec as P
+
+ORDER = ("x", "y", "row")
 
 
 def spread(value, axis, root):
@@ -9,14 +16,14 @@
     return lax.psum(jnp.where(mine, value, jnp.zeros_like(value)), axis)
 
 
-def layer_norm(values):
-    mean = jnp.mean(values, axis=-1, keepdims=True)
+def layer_norm(values, axis=-1):
+    mean = jnp.mean(values, axis=axis, keepdims=True)
     centred = values - mean
-    var = jnp.mean(centred * centred, axis=-1, keepdims=True)
+    var = jnp.mean(centred * centred, axis=axis, keepdims=True)
     return centred * jax.lax.rsqrt(var + 1e-05)
 
 
-def body(pair, pair_mask, in_weights, gate_weight, out_weight):
+def gather_rows(pair, pair_mask, in_weights, gate_weight, out_weight):
     rows_here = pair.shape[0]
     cols_here = pair.shape[1]
     width = pair.shape[2]
@@ -47,7 +54,225 @@
     return update.astype(jnp.bfloat16).reshape(rows_here, cols_here, width)
 
 
+def sigmoid(values):
+    return 0.5 * jnp.tanh(0.5 * values) + 0.5
+
+
+def project_kernel(
+    devices, mine, cols_here,
+    pair_hbm, mask_hbm, weights_hbm, send_ref, normed_ref, pair_ref, mask_ref, weights_ref, done,
+):
+    spots = pair_ref.shape[0]
+    hidden = devices * mine
+    parts = 4
+    copies = []
+    for part in range(parts):
+        lanes = pl.ds(part * hidden, hidden)
+        copies.append((weights_hbm.at[:, lanes], weights_ref.at[:, lanes]))
+    copies.append((mask_hbm, mask_ref))
+    for part in range(parts):
+        some = pl.ds(part * spots // parts, spots // parts)
+        copies.append((pair_hbm.at[some], pair_ref.at[some]))
+    copies = [pltpu.make_async_copy(*ends, done.at[n]) for n, ends in enumerate(copies)]
+    for copy in copies:
+        copy.start()
+    shape = (2 * hidden, 2 * hidden)
+    row, col = (lax.broadcasted_iota(jnp.int32, shape, n) for n in (0, 1))
+    source = (row // mine) % 2 * hidden + row // (2 * mine) * mine + row % mine
+    order = (col == source).astype(jnp.bfloat16)
+    for copy in copies[:parts]:
+        copy.wait()
+    weights = weights_ref[...]
+
+    def in_order(block):
+        both = [weights[:, (block + n) * hidden : (block + n + 1) * hidden] for n in (0, 2)]
+        return dot_t(order, jnp.concatenate(both, axis=1)).astype(jnp.bfloat16)
+
+    values, gates = in_order(0), in_order(1)
+    shape = (cols_here, spots)
+    row, col = (lax.broadcasted_iota(jnp.int32, shape, n) for n in (0, 1))
+    spread_cols = (col % cols_here == row).astype(jnp.bfloat16)
+    copies[parts].wait()
+    mask = mask_ref[...].astype(jnp.float32).astype(jnp.bfloat16)
+    mask = jnp.dot(mask, spread_cols, preferred_element_type=jnp.float32)
+    row, col = (lax.broadcasted_iota(jnp.int32, mask.shape, n) for n in (0, 1))
+    mask = jnp.sum(jnp.where(col // cols_here == row, mask, 0.0), axis=0, keepdims=True)
+    for copy in copies[parts + 1 :]:
+        copy.wait()
+    normed = layer_norm(pair_ref[...].astype(jnp.float32)).astype(jnp.bfloat16)
+    normed_ref[...] = normed
+    both = mask * sigmoid(dot_t(gates, normed)) * dot_t(values, normed)
+    both = both.reshape(devices, 2 * mine, spots)
+    half = spots // 2
+    both = jnp.concatenate([both[:, :, :half], both[:, :, half:]], axis=1)
+    send_ref[...] = both.astype(jnp.bfloat16)
+
+
+def dot_t(a, b):
+    return lax.dot_general(a, b, (((1,), (1,)), ((), ())), preferred_element_type=jnp.float32)
+
+
+def swap_groups(tiles):
+    lane = lax.broadcasted_iota(jnp.int32, tiles[0].shape, 1)
+    width = tiles[0].shape[1]
+    half, quarter = width // 2, width // 4
+    low, even = lane < half, lane // quarter % 2 == 0
+    a = [
+        jnp.where(low, tiles[0], pltpu.roll(tiles[2], half, 1)),
+        jnp.where(low, tiles[1], pltpu.roll(tiles[3], half, 1)),
+        jnp.where(low, pltpu.roll(tiles[0], half, 1), tiles[2]),
+        jnp.where(low, pltpu.roll(tiles[1], half, 1), tiles[3]),
+    ]
+    return [
+        jnp.where(even, a[0], pltpu.roll(a[1], quarter, 1)),
+        jnp.where(even, pltpu.roll(a[0], width - quarter, 1), a[1]),
+        jnp.where(even, a[2], pltpu.roll(a[3], quarter, 1)),
+        jnp.where(even, pltpu.roll(a[2], width - quarter, 1), a[3]),
+    ]
+
+
+NEAR, FAR, WIDE = 9, 17, 137
+
+
+def mix_kernel(places, mine, recv_ref, send_ref, got, partner, back):
+    rows = len(places[0])
+    depth = 4 * mine
+    for col, column in enumerate(places):
+        for row, place in enumerate(column):
+            block = recv_ref[place].astype(jnp.float32)
+            for high in range(2):
+                for middle in range(2):
+                    tile = block[8 * high : 8 * high + 8, 128 * middle : 128 * middle + 128]
+                    got[col, 2 * high + middle, pl.ds(NEAR * row, 8, stride=FAR), :] = tile
+
+    def side(which, channel):
+        first = FAR * (which * mine + channel)
+        tiles = []
+        for high in range(4):
+            some = pl.ds(first, rows, stride=NEAR)
+            tiles += swap_groups([got[col, high, some, :] for col in range(len(places))])
+        return tiles
+
+    for channel in range(mine):
+        left = jnp.concatenate(side(0, channel), axis=0).astype(jnp.bfloat16)
+        for n, tile in enumerate(side(1, channel)):
+            partner[channel, pl.ds(NEAR * n, rows, stride=WIDE), :] = tile
+        right = [
+            partner[channel, pl.ds(WIDE * row + NEAR * n, 8, stride=NEAR), :]
+            for row in range(rows)
+            for n in (0, 8)
+        ]
+        tri = dot_t(left, jnp.concatenate(right, axis=0).astype(jnp.bfloat16))
+        for high in range(4):
+            tiles = [tri[(4 * high + n) * rows : (4 * high + n + 1) * rows] for n in range(4)]
+            for col, tile in enumerate(swap_groups(tiles)):
+                first = NEAR * (high * mine + channel)
+                back[col, pl.ds(first, rows, stride=WIDE), :] = tile
+    for col, column in enumerate(places):
+        for row, place in enumerate(column):
+            tiles = [
+                back[col, pl.ds(WIDE * row + NEAR * n, 8, stride=NEAR), :]
+                for n in range(0, depth, 8)
+            ]
+            send_ref[place] = jnp.concatenate(tiles, axis=0).astype(jnp.bfloat16)
+
+
+def finish_kernel(recv_ref, gate_ref, weight_ref, out_hbm, out_ref, done):
+    devices, depth, width = recv_ref.shape
+    values = recv_ref[...].astype(jnp.float32).reshape(devices // 2, 2, depth // 8, 8, width)
+    top = lax.broadcasted_iota(jnp.int32, (devices // 2, 8, width), 1) < 4
+    weight = weight_ref[...]
+    parts = []
+    for n in range(depth // 8):
+        one, two = values[:, 0, n], values[:, 1, n]
+        parts.append(jnp.where(top, one, pltpu.roll(two, 4, 1)))
+        parts.append(jnp.where(top, pltpu.roll(one, 4, 1), two))
+    copies = []
+    for n, part in enumerate(parts):
+        part = layer_norm(part.reshape(devices * 4, width), axis=0)
+        tnorm = part.T.astype(jnp.bfloat16)
+        update = jnp.dot(tnorm, weight, preferred_element_type=jnp.float32)
+        spots = pl.ds(n * width, width)
+        out_ref[spots, :] = (gate_ref[spots, :] * update).astype(jnp.bfloat16)
+        copies.append(pltpu.make_async_copy(out_ref.at[spots], out_hbm.at[spots], done.at[n]))
+        copies[-1].start()
+    for copy in copies:
+        copy.wait()
+
+
+def in_hbm(values):
+    return pltpu.with_memory_space_constraint(values, pltpu.HBM)
+
+
+def split_channels(pair, pair_mask, in_weights, gate_weight, out_weight):
+    rows_here, cols_here, width = pair.shape
+    hidden = in_weights.shape[1] // 4
+    sizes = {name: lax.axis_size(name) for name in ORDER}
+    steps = {name: math.prod([sizes[n] for n in ORDER[at + 1 :]]) for at, name in enumerate(ORDER)}
+    rows, cols = sizes["row"], sizes["y"] * sizes["x"]
+    firsts = [y * steps["y"] + x * steps["x"] for y in range(sizes["y"]) for x in range(sizes["x"])]
+    devices = rows * cols
+    mine = hidden // devices
+    spots = rows_here * cols_here
+    params = pltpu.CompilerParams(vmem_limit_bytes=32 * 2**20)
+    both, normed = pl.pallas_call(
+        functools.partial(project_kernel, devices, mine, cols_here),
+        out_shape=(
+            jax.ShapeDtypeStruct((devices, 4 * mine, spots // 2), jnp.bfloat16),
+            jax.ShapeDtypeStruct((spots, width), jnp.bfloat16),
+        ),
+        in_specs=[pl.BlockSpec(memory_space=pltpu.HBM)] * 3,
+        scratch_shapes=[
+            pltpu.VMEM((spots, width), pair.dtype),
+            pltpu.VMEM(pair_mask.shape, pair_mask.dtype),
+            pltpu.VMEM(in_weights.shape, in_weights.dtype),
+            pltpu.SemaphoreType.DMA((9,)),
+        ],
+        compiler_params=params,
+        name="project",
+    )(*(in_hbm(values) for values in (pair.reshape(spots, width), pair_mask, in_weights)))
+    both = lax.all_to_all(both, ORDER, 0, 0, tiled=True)
+    gate = sigmoid(jnp.dot(normed, gate_weight, preferred_element_type=jnp.float32))
+    places = [[first + row * steps["row"] for row in range(rows)] for first in firsts]
+    tri = pl.pallas_call(
+        functools.partial(mix_kernel, places, mine),
+        out_shape=jax.ShapeDtypeStruct((devices, 4 * mine, spots // 4), jnp.bfloat16),
+        scratch_shapes=[
+            pltpu.VMEM((cols, 4, 184, 128), jnp.float32),
+            pltpu.VMEM((mine, 1096, 128), jnp.float32),
+            pltpu.VMEM((cols, 1096, 128), jnp.float32),
+        ],
+        compiler_params=params,
+        name="mix",
+    )(both)
+    tri = lax.all_to_all(tri, ORDER, 0, 0, tiled=True)
+    update = pl.pallas_call(
+        finish_kernel,
+        out_shape=jax.ShapeDtypeStruct((spots, width), jnp.bfloat16),
+        out_specs=pl.BlockSpec(memory_space=pltpu.HBM),
+        scratch_shapes=[pltpu.VMEM((spots, width), jnp.bfloat16), pltpu.SemaphoreType.DMA((4,))],
+        compiler_params=params,
+        name="finish",
+    )(tri, gate, out_weight)
+    return update.reshape(rows_here, cols_here, width)
+
+
+def fits(rows, cols, pair, hidden):
+    sizes = (rows, cols, pair.shape[0] // rows, pair.shape[1] // cols, pair.shape[2])
+    return sizes == (8, 4, 16, 32, 128) and hidden == 4 * rows * cols
+
+
 def solution(mesh):
-    in_specs = (P("row", "col", None), P("row", "col"), P(), P(), P())
-    out_specs = P("row", "col", None)
-    return jax.shard_map(body, mesh=mesh, in_specs=in_specs, out_specs=out_specs, check_vma=False)
+    def update(pair, pair_mask, in_weights, gate_weight, out_weight):
+        rows, cols = mesh.shape["row"], mesh.shape["col"]
+        if fits(rows, cols, pair, in_weights.shape[1] // 4):
+            plan, col = split_channels, ("y", "x")
+            over = jax.sharding.Mesh(mesh.devices.reshape(rows, 2, 2), ("row", *col))
+        else:
+            plan, col, over = gather_rows, "col", mesh
+        in_specs = (P("row", col, None), P("row", col), P(), P(), P())
+        out_specs = P("row", col, None)
+        run = jax.shard_map(plan, mesh=over, in_specs=in_specs, out_specs=out_specs, check_vma=False)
+        return run(pair, pair_mask, in_weights, gate_weight, out_weight)
+
+    return update

time: 95.3 us -> 32.6 us (0.34)
  waiting for transfers between devices: 48.3 us -> 7.96 us
  between operations: 13.5 us -> 0.04 us
  other arithmetic: 5.74 us -> 0 us
  blocking collectives: 21.7 us -> 17.5 us
  Pallas kernels: 0 us -> 4.07 us
  matrix products: 3.17 us -> 0.18 us
  local copies, waits for them, and re-layouts: 2.59 us -> 0.01 us
  starting transfers between devices: 0.01 us -> 2.58 us
    psum x1 -> x0, waiting for transfers between devices: 48.2 us -> none  [spread(): return lax.psum(jnp.where(mine, value, jnp.zeros_like(value)), axis)]
    all_gather x2 -> x0, blocking collectives: 21.7 us -> none  [the longest x1 11.5 us: body(): lax.all_gather(right, 'col', axis=1, tiled=True)]
    all_to_all x0 -> x1, blocking collectives: none -> 17.5 us  [split_channels(): both = lax.all_to_all(both, ORDER, 0, 0, tiled=True)]
    all_to_all x0 -> x1, waiting for transfers between devices: none -> 7.96 us  [split_channels(): tri = lax.all_to_all(tri, ORDER, 0, 0, tiled=True)]
    pallas_call x0 -> x3, Pallas kernels: none -> 4.07 us  [the longest x1 1.76 us: split_channels(): pl.pallas_call(functools.partial(project_kernel, devices, mine, cols_here...]
    dot_general x4 -> x1, matrix products: 3.17 us -> 0.18 us  [split_channels(): jnp.dot(normed, gate_weight, preferred_element_type=jnp.float32)]
    all_to_all x0 -> x1, starting transfers between devices: none -> 2.58 us  [split_channels(): tri = lax.all_to_all(tri, ORDER, 0, 0, tiled=True)]
    reduce_sum x3 -> x0, other arithmetic: 2.43 us -> none  [the longest x2 1.35 us: layer_norm(): var = jnp.mean(centred * centred, axis=-1, keepdims=True)]
where the time goes in v1:
time: 32.6 us; the launch traced here: 32.3 us
  blocking collectives  17.5 us (54%)
  waiting for transfers between devices  7.96 us (24%)
  Pallas kernels  4.07 us (12%)
  starting transfers between devices  2.58 us (8%)
    all_to_all x1, blocking collectives, split_channels(): both = lax.all_to_all(both, ORDER, 0, 0, tiled=True)  17.5 us
    all_to_all x1, waiting for transfers between devices, split_channels(): tri = lax.all_to_all(tri, ORDER, 0, 0, tiled=True)  7.96 us
    all_to_all x1, starting transfers between devices, split_channels(): tri = lax.all_to_all(tri, ORDER, 0, 0, tiled=True)  2.58 us
    pallas_call x1, Pallas kernels, split_channels(): pl.pallas_call(functools.partial(project_kernel, devices, mine, cols_here...  1.76 us
    pallas_call x1, Pallas kernels, split_channels(): pl.pallas_call(functools.partial(mix_kernel, places, mine), out_shape=jax...  1.31 us
    pallas_call x1, Pallas kernels, split_channels(): pl.pallas_call(finish_kernel, out_shape=jax.ShapeDtypeStruct((spots, widt...  1 us
  transfers between devices with their start and end apart: 1, of which 1 were waited for; matrix products, arithmetic and copies ran while one was open for 1% of the time, Pallas kernels for 0%

profile of v1, /device:TPU:0, one launch (start us, length us, event | category | flops | bytes accessed | tf_op | source)
XLA Modules:
  0.0 32.3 jit_solution(2969543080748968032)
XLA Ops:
  0.0 0.0 copy-start
  0.0 1.8 %project.1 = (bf16[32,16,256]{2,1,0:T(8,128)(2,1)S(1)}, bf16[512,128]{1,0:T(8,128)(2,1)S(1)}) custom-call(bf16[512,128]{1,0:T(8,128)(2,1)} %bitcast.4, s32[16,32]{1,0:T(8,128)} %mask_hbm.1, bf16[128,512]{1,0:T(8,128)(2,1)} %weights_hbm.1), custom_call_target="tpu_custom_call" | custom-call | tf_op jit(solution)/shard_map/project/pallas_call | solution.py:218
  1.8 17.5 %all_to_all.10.recv_ref = bf16[32,16,256]{2,1,0:T(8,128)(2,1)S(1)} all-to-all(bf16[32,16,256]{2,1,0:T(8,128)(2,1)S(1)} %get-tuple-element.7), channel_id=1, replica_groups=mesh['row'=8,'y'=2,'x'=2] {'x','y','row'}, dimensions={0} | all-to-all | bytes 524288 | tf_op jit(solution)/shard_map/all_to_all | solution.py:234
  19.3 1.3 %mix.1 = bf16[32,16,128]{2,1,0:T(8,128)(2,1)} custom-call(bf16[32,16,256]{2,1,0:T(8,128)(2,1)S(1)} %all_to_all.10.recv_ref), custom_call_target="tpu_custom_call" | custom-call | tf_op jit(solution)/shard_map/mix/pallas_call | solution.py:237
  20.6 2.6 %all-to-all-start.1 = ((bf16[32,16,128]{2,1,0:T(8,128)(2,1)}), bf16[32,16,128]{2,1,0:T(8,128)(2,1)S(1)}, u32[]{:S(2)}, u32[]{:S(2)}) async-start(bf16[32,16,128]{2,1,0:T(8,128)(2,1)} %mix.1), calls=%async_computation.1 | async-start | bytes 262144 | tf_op jit(solution)/shard_map/all_to_all | solution.py:248
  23.2 0.0 copy-done
  23.2 0.0 copy-start.1
  23.2 0.2 fusion.2.gate_ref
  23.4 8.0 %all-to-all-done.1.recv_ref = bf16[32,16,128]{2,1,0:T(8,128)(2,1)S(1)} async-done(((bf16[32,16,128]{2,1,0:T(8,128)(2,1)}), bf16[32,16,128]{2,1,0:T(8,128)(2,1)S(1)}, u32[]{:S(2)}, u32[]{:S(2)}) %all-to-all-start.1) | async-done | bytes 131104 | tf_op jit(solution)/shard_map/all_to_all | solution.py:248
  31.3 0.0 copy-done.1
  31.3 1.0 %finish.1 = bf16[512,128]{1,0:T(8,128)(2,1)} custom-call(bf16[32,16,128]{2,1,0:T(8,128)(2,1)S(1)} %all-to-all-done.1.recv_ref, f32[512,128]{1,0:T(8,128)S(1)} %fusion.2.gate_ref, bf16[128,128]{1,0:T(8,128)(2,1)S(1)} %copy-done.1), custom_call_target="tpu_custom_call" | custom-call | tf_op jit(solution)/shard_map/finish/pallas_call | solution.py:249
Async XLA Ops:
  0.0 23.2 %copy-start = (bf16[128,128]{1,0:T(8,128)(2,1)S(1)}, bf16[128,128]{1,0:T(8,128)(2,1)}, u32[]{:S(2)}) copy-start(bf16[128,128]{1,0:T(8,128)(2,1)} %param.8) | copy-start | bytes 98308
  20.6 10.8 %all-to-all-start.1 = ((bf16[32,16,128]{2,1,0:T(8,128)(2,1)}), bf16[32,16,128]{2,1,0:T(8,128)(2,1)S(1)}, u32[]{:S(2)}, u32[]{:S(2)}) async-start(bf16[32,16,128]{2,1,0:T(8,128)(2,1)} %mix.1), calls=%async_computation.1 | async-start | bytes 262144 | tf_op jit(solution)/shard_map/all_to_all | solution.py:248
  23.2 8.2 %copy-start.1 = (bf16[128,128]{1,0:T(8,128)(2,1)S(1)}, bf16[128,128]{1,0:T(8,128)(2,1)}, u32[]{:S(2)}) copy-start(bf16[128,128]{1,0:T(8,128)(2,1)} %weight_ref.1) | copy-start | bytes 98308

commit v2 on v1

--- a/solution.py
+++ b/solution.py
@@ -62,17 +62,13 @@
     devices, mine, cols_here,
     pair_hbm, mask_hbm, weights_hbm, send_ref, normed_ref, pair_ref, mask_ref, weights_ref, done,
 ):
-    spots = pair_ref.shape[0]
+    spots, width = pair_ref.shape
     hidden = devices * mine
-    parts = 4
     copies = []
-    for part in range(parts):
-        lanes = pl.ds(part * hidden, hidden)
-        copies.append((weights_hbm.at[:, lanes], weights_ref.at[:, lanes]))
+    for source, target in ((pair_hbm, pair_ref), (weights_hbm, weights_ref)):
+        half = source.shape[0] // 2
+        copies += [(source.at[pl.ds(n, half)], target.at[pl.ds(n, half)]) for n in (0, half)]
     copies.append((mask_hbm, mask_ref))
-    for part in range(parts):
-        some = pl.ds(part * spots // parts, spots // parts)
-        copies.append((pair_hbm.at[some], pair_ref.at[some]))
     copies = [pltpu.make_async_copy(*ends, done.at[n]) for n, ends in enumerate(copies)]
     for copy in copies:
         copy.start()
@@ -80,7 +76,17 @@
     row, col = (lax.broadcasted_iota(jnp.int32, shape, n) for n in (0, 1))
     source = (row // mine) % 2 * hidden + row // (2 * mine) * mine + row % mine
     order = (col == source).astype(jnp.bfloat16)
-    for copy in copies[:parts]:
+    shape = (cols_here, spots)
+    row, col = (lax.broadcasted_iota(jnp.int32, shape, n) for n in (0, 1))
+    spread_cols = (col % cols_here == row).astype(jnp.bfloat16)
+    shape = (spots // cols_here, spots)
+    row, col = (lax.broadcasted_iota(jnp.int32, shape, n) for n in (0, 1))
+    own = col // cols_here == row
+    for copy in copies[:2]:
+        copy.wait()
+    normed = layer_norm(pair_ref[...].astype(jnp.float32)).astype(jnp.bfloat16)
+    normed_ref[...] = normed
+    for copy in copies[2:]:
         copy.wait()
     weights = weights_ref[...]
 
@@ -88,20 +94,10 @@
         both = [weights[:, (block + n) * hidden : (block + n + 1) * hidden] for n in (0, 2)]
         return dot_t(order, jnp.concatenate(both, axis=1)).astype(jnp.bfloat16)
 
-    values, gates = in_order(0), in_order(1)
-    shape = (cols_here, spots)
-    row, col = (lax.broadcasted_iota(jnp.int32, shape, n) for n in (0, 1))
-    spread_cols = (col % cols_here == row).astype(jnp.bfloat16)
-    copies[parts].wait()
     mask = mask_ref[...].astype(jnp.float32).astype(jnp.bfloat16)
     mask = jnp.dot(mask, spread_cols, preferred_element_type=jnp.float32)
-    row, col = (lax.broadcasted_iota(jnp.int32, mask.shape, n) for n in (0, 1))
-    mask = jnp.sum(jnp.where(col // cols_here == row, mask, 0.0), axis=0, keepdims=True)
-    for copy in copies[parts + 1 :]:
-        copy.wait()
-    normed = layer_norm(pair_ref[...].astype(jnp.float32)).astype(jnp.bfloat16)
-    normed_ref[...] = normed
-    both = mask * sigmoid(dot_t(gates, normed)) * dot_t(values, normed)
+    mask = jnp.sum(jnp.where(own, mask, 0.0), axis=0, keepdims=True)
+    both = mask * sigmoid(dot_t(in_order(1), normed)) * dot_t(in_order(0), normed)
     both = both.reshape(devices, 2 * mine, spots)
     half = spots // 2
     both = jnp.concatenate([both[:, :, :half], both[:, :, half:]], axis=1)
@@ -146,28 +142,43 @@
                     got[col, 2 * high + middle, pl.ds(NEAR * row, 8, stride=FAR), :] = tile
 
     def side(which, channel):
-        first = FAR * (which * mine + channel)
+        some = pl.ds(FAR * (which * mine + channel), rows, stride=NEAR)
         tiles = []
-        for high in range(4):
-            some = pl.ds(first, rows, stride=NEAR)
-            tiles += swap_groups([got[col, high, some, :] for col in range(len(places))])
+        for middle in range(2):
+            some_of = [
+                jnp.concatenate([got[col, middle, some, :], got[col, 2 + middle, some, :]], axis=0)
+                for col in range(len(places))
+            ]
+            tiles += swap_groups([tile.astype(jnp.bfloat16) for tile in some_of])
         return tiles
 
-    for channel in range(mine):
-        left = jnp.concatenate(side(0, channel), axis=0).astype(jnp.bfloat16)
+    def spread_rows(target, first, step, tile):
+        tile = tile.astype(jnp.float32)
+        for high in range(2):
+            some = pl.ds(NEAR * (first + high * step), rows, stride=WIDE)
+            target[some, :] = tile[high * rows : (high + 1) * rows]
+
+    channels = range(mine)
+    for channel in channels:
         for n, tile in enumerate(side(1, channel)):
-            partner[channel, pl.ds(NEAR * n, rows, stride=WIDE), :] = tile
-        right = [
+            spread_rows(partner.at[channel], n, 8, tile)
+    lefts = [jnp.concatenate(side(0, channel), axis=0) for channel in channels]
+    rights = [
+        [
             partner[channel, pl.ds(WIDE * row + NEAR * n, 8, stride=NEAR), :]
             for row in range(rows)
             for n in (0, 8)
         ]
-        tri = dot_t(left, jnp.concatenate(right, axis=0).astype(jnp.bfloat16))
-        for high in range(4):
-            tiles = [tri[(4 * high + n) * rows : (4 * high + n + 1) * rows] for n in range(4)]
-            for col, tile in enumerate(swap_groups(tiles)):
-                first = NEAR * (high * mine + channel)
-                back[col, pl.ds(first, rows, stride=WIDE), :] = tile
+        for channel in channels
+    ]
+    rights = [jnp.concatenate(right, axis=0).astype(jnp.bfloat16) for right in rights]
+    tris = [dot_t(left, right).astype(jnp.bfloat16) for left, right in zip(lefts, rights)]
+    for channel, tri in enumerate(tris):
+        for middle in range(2):
+            firsts = [(4 * middle + n) * 2 * rows for n in range(4)]
+            tiles = swap_groups([tri[first : first + 2 * rows] for first in firsts])
+            for col, tile in enumerate(tiles):
+                spread_rows(back.at[col], middle * mine + channel, 2 * mine, tile)
     for col, column in enumerate(places):
         for row, place in enumerate(column):
             tiles = [
@@ -177,11 +188,14 @@
             send_ref[place] = jnp.concatenate(tiles, axis=0).astype(jnp.bfloat16)
 
 
-def finish_kernel(recv_ref, gate_ref, weight_ref, out_hbm, out_ref, done):
+def finish_kernel(recv_ref, normed_ref, gate_weight_ref, weight_ref, out_hbm, out_ref, done):
     devices, depth, width = recv_ref.shape
     values = recv_ref[...].astype(jnp.float32).reshape(devices // 2, 2, depth // 8, 8, width)
     top = lax.broadcasted_iota(jnp.int32, (devices // 2, 8, width), 1) < 4
     weight = weight_ref[...]
+    gate = sigmoid(
+        jnp.dot(normed_ref[...], gate_weight_ref[...], preferred_element_type=jnp.float32)
+    )
     parts = []
     for n in range(depth // 8):
         one, two = values[:, 0, n], values[:, 1, n]
@@ -193,9 +207,11 @@
         tnorm = part.T.astype(jnp.bfloat16)
         update = jnp.dot(tnorm, weight, preferred_element_type=jnp.float32)
         spots = pl.ds(n * width, width)
-        out_ref[spots, :] = (gate_ref[spots, :] * update).astype(jnp.bfloat16)
+        out_ref[spots, :] = (gate[n * width : (n + 1) * width] * update).astype(jnp.bfloat16)
         copies.append(pltpu.make_async_copy(out_ref.at[spots], out_hbm.at[spots], done.at[n]))
-        copies[-1].start()
+        if n % 2:
+            copies[n - 1].start()
+            copies[n].start()
     for copy in copies:
         copy.wait()
 
@@ -226,13 +242,12 @@
             pltpu.VMEM((spots, width), pair.dtype),
             pltpu.VMEM(pair_mask.shape, pair_mask.dtype),
             pltpu.VMEM(in_weights.shape, in_weights.dtype),
-            pltpu.SemaphoreType.DMA((9,)),
+            pltpu.SemaphoreType.DMA((5,)),
         ],
         compiler_params=params,
         name="project",
     )(*(in_hbm(values) for values in (pair.reshape(spots, width), pair_mask, in_weights)))
     both = lax.all_to_all(both, ORDER, 0, 0, tiled=True)
-    gate = sigmoid(jnp.dot(normed, gate_weight, preferred_element_type=jnp.float32))
     places = [[first + row * steps["row"] for row in range(rows)] for first in firsts]
     tri = pl.pallas_call(
         functools.partial(mix_kernel, places, mine),
@@ -253,7 +268,7 @@
         scratch_shapes=[pltpu.VMEM((spots, width), jnp.bfloat16), pltpu.SemaphoreType.DMA((4,))],
         compiler_params=params,
         name="finish",
-    )(tri, gate, out_weight)
+    )(tri, normed, gate_weight, out_weight)
     return update.reshape(rows_here, cols_here, width)
 
 

time: 32.6 us -> 31.6 us (0.969)
  blocking collectives: 17.5 us -> 28 us
  waiting for transfers between devices: 7.96 us -> 0 us
  starting transfers between devices: 2.58 us -> 0 us
  Pallas kernels: 4.07 us -> 3.37 us
    all_to_all x0 -> x1, blocking collectives: none -> 10.5 us  [split_channels(): tri = lax.all_to_all(tri, ORDER, 0, 0, tiled=True)]
    all_to_all x1 -> x0, waiting for transfers between devices: 7.96 us -> none  [split_channels(): tri = lax.all_to_all(tri, ORDER, 0, 0, tiled=True)]
    all_to_all x1 -> x0, starting transfers between devices: 2.58 us -> none  [split_channels(): tri = lax.all_to_all(tri, ORDER, 0, 0, tiled=True)]
    pallas_call x1, Pallas kernels: 1.31 us -> 0.62 us  [split_channels(): pl.pallas_call(functools.partial(mix_kernel, places, mine), out_shape=jax...]
  transfers between devices with their start and end apart: 1 -> 0, of which waited for: 1 -> 0; matrix products, arithmetic and copies ran while one was open for 1% -> 0% of each run, Pallas kernels for 0% -> 0%
where the time goes in v2:
time: 31.6 us; the launch traced here: 31.4 us
  blocking collectives  28 us (89%)
  Pallas kernels  3.37 us (11%)
    all_to_all x1, blocking collectives, split_channels(): both = lax.all_to_all(both, ORDER, 0, 0, tiled=True)  17.5 us
    all_to_all x1, blocking collectives, split_channels(): tri = lax.all_to_all(tri, ORDER, 0, 0, tiled=True)  10.5 us
    pallas_call x1, Pallas kernels, split_channels(): pl.pallas_call(functools.partial(project_kernel, devices, mine, cols_here...  1.74 us
    pallas_call x1, Pallas kernels, split_channels(): pl.pallas_call(finish_kernel, out_shape=jax.ShapeDtypeStruct((spots, widt...  1.01 us

profile of v2, /device:TPU:0, one launch (start us, length us, event | category | flops | bytes accessed | tf_op | source)
XLA Modules:
  0.0 31.4 jit_solution(3439365368006135712)
XLA Ops:
  0.0 1.7 %project.1 = (bf16[32,16,256]{2,1,0:T(8,128)(2,1)S(1)}, bf16[512,128]{1,0:T(8,128)(2,1)S(1)}) custom-call(bf16[512,128]{1,0:T(8,128)(2,1)} %bitcast.2, s32[16,32]{1,0:T(8,128)} %mask_hbm.1, bf16[128,512]{1,0:T(8,128)(2,1)} %weights_hbm.1), custom_call_target="tpu_custom_call" | custom-call | tf_op jit(solution)/shard_map/project/pallas_call | solution.py:234
  1.7 17.5 %all_to_all.10.recv_ref = bf16[32,16,256]{2,1,0:T(8,128)(2,1)S(1)} all-to-all(bf16[32,16,256]{2,1,0:T(8,128)(2,1)S(1)} %get-tuple-element.7), channel_id=1, replica_groups=mesh['row'=8,'y'=2,'x'=2] {'x','y','row'}, dimensions={0} | all-to-all | bytes 524288 | tf_op jit(solution)/shard_map/all_to_all | solution.py:250
  19.2 0.6 %mix.1 = bf16[32,16,128]{2,1,0:T(8,128)(2,1)S(1)} custom-call(bf16[32,16,256]{2,1,0:T(8,128)(2,1)S(1)} %all_to_all.10.recv_ref), custom_call_target="tpu_custom_call" | custom-call | tf_op jit(solution)/shard_map/mix/pallas_call | solution.py:252
  19.9 0.0 copy-start
  19.9 0.0 copy-start.1
  19.9 10.5 %all_to_all.11.recv_ref = bf16[32,16,128]{2,1,0:T(8,128)(2,1)S(1)} all-to-all(bf16[32,16,128]{2,1,0:T(8,128)(2,1)S(1)} %mix.1), channel_id=1, replica_groups=mesh['row'=8,'y'=2,'x'=2] {'x','y','row'}, dimensions={0} | all-to-all | bytes 262144 | tf_op jit(solution)/shard_map/all_to_all | solution.py:263
  30.4 0.0 copy-done
  30.4 0.0 copy-done.1
  30.4 1.0 %finish.1 = bf16[512,128]{1,0:T(8,128)(2,1)} custom-call(bf16[32,16,128]{2,1,0:T(8,128)(2,1)S(1)} %all_to_all.11.recv_ref, bf16[512,128]{1,0:T(8,128)(2,1)S(1)} %get-tuple-element.8.normed_ref, bf16[128,128]{1,0:T(8,128)(2,1)S(1)} %copy-done, bf16[128,128]{1,0:T(8,128)(2,1)S(1)} %copy-done.1), custom_call_target="tpu_custom_call" | custom-call | tf_op jit(solution)/shard_map/finish/pallas_call | solution.py:264
Async XLA Ops:
  19.9 10.5 %copy-start = (bf16[128,128]{1,0:T(8,128)(2,1)S(1)}, bf16[128,128]{1,0:T(8,128)(2,1)}, u32[]{:S(2)}) copy-start(bf16[128,128]{1,0:T(8,128)(2,1)} %gate_weight_ref.1) | copy-start | bytes 98308
  19.9 10.5 %copy-start.1 = (bf16[128,128]{1,0:T(8,128)(2,1)S(1)}, bf16[128,128]{1,0:T(8,128)(2,1)}, u32[]{:S(2)}) copy-start(bf16[128,128]{1,0:T(8,128)(2,1)} %weight_ref.1) | copy-start | bytes 98308

commit v3 on v2

--- a/solution.py
+++ b/solution.py
@@ -8,7 +8,7 @@
 from jax.experimental.pallas import tpu as pltpu
 from jax.sharding import PartitionSpec as P
 
-ORDER = ("x", "y", "row")
+ORDER = ("core", "x", "y", "z")
 
 
 def spread(value, axis, root):
@@ -64,11 +64,10 @@
 ):
     spots, width = pair_ref.shape
     hidden = devices * mine
-    copies = []
-    for source, target in ((pair_hbm, pair_ref), (weights_hbm, weights_ref)):
+    copies = [(mask_hbm, mask_ref)]
+    for source, target in ((weights_hbm, weights_ref), (pair_hbm, pair_ref)):
         half = source.shape[0] // 2
         copies += [(source.at[pl.ds(n, half)], target.at[pl.ds(n, half)]) for n in (0, half)]
-    copies.append((mask_hbm, mask_ref))
     copies = [pltpu.make_async_copy(*ends, done.at[n]) for n, ends in enumerate(copies)]
     for copy in copies:
         copy.start()
@@ -82,11 +81,7 @@
     shape = (spots // cols_here, spots)
     row, col = (lax.broadcasted_iota(jnp.int32, shape, n) for n in (0, 1))
     own = col // cols_here == row
-    for copy in copies[:2]:
-        copy.wait()
-    normed = layer_norm(pair_ref[...].astype(jnp.float32)).astype(jnp.bfloat16)
-    normed_ref[...] = normed
-    for copy in copies[2:]:
+    for copy in copies:
         copy.wait()
     weights = weights_ref[...]
 
@@ -97,6 +92,8 @@
     mask = mask_ref[...].astype(jnp.float32).astype(jnp.bfloat16)
     mask = jnp.dot(mask, spread_cols, preferred_element_type=jnp.float32)
     mask = jnp.sum(jnp.where(own, mask, 0.0), axis=0, keepdims=True)
+    normed = layer_norm(pair_ref[...].astype(jnp.float32)).astype(jnp.bfloat16)
+    normed_ref[...] = normed
     both = mask * sigmoid(dot_t(in_order(1), normed)) * dot_t(in_order(0), normed)
     both = both.reshape(devices, 2 * mine, spots)
     half = spots // 2
@@ -209,9 +206,8 @@
         spots = pl.ds(n * width, width)
         out_ref[spots, :] = (gate[n * width : (n + 1) * width] * update).astype(jnp.bfloat16)
         copies.append(pltpu.make_async_copy(out_ref.at[spots], out_hbm.at[spots], done.at[n]))
-        if n % 2:
-            copies[n - 1].start()
-            copies[n].start()
+    for copy in copies:
+        copy.start()
     for copy in copies:
         copy.wait()
 
@@ -225,8 +221,14 @@
     hidden = in_weights.shape[1] // 4
     sizes = {name: lax.axis_size(name) for name in ORDER}
     steps = {name: math.prod([sizes[n] for n in ORDER[at + 1 :]]) for at, name in enumerate(ORDER)}
-    rows, cols = sizes["row"], sizes["y"] * sizes["x"]
-    firsts = [y * steps["y"] + x * steps["x"] for y in range(sizes["y"]) for x in range(sizes["x"])]
+
+    def offsets(slow, fast):
+        pairs = [(m, n) for m in range(sizes[slow]) for n in range(sizes[fast])]
+        return [m * steps[slow] + n * steps[fast] for m, n in pairs]
+
+    in_rows, in_cols = offsets("z", "core"), offsets("y", "x")
+    places = [[first + row for row in in_rows] for first in in_cols]
+    rows, cols = len(in_rows), len(in_cols)
     devices = rows * cols
     mine = hidden // devices
     spots = rows_here * cols_here
@@ -248,7 +250,6 @@
         name="project",
     )(*(in_hbm(values) for values in (pair.reshape(spots, width), pair_mask, in_weights)))
     both = lax.all_to_all(both, ORDER, 0, 0, tiled=True)
-    places = [[first + row * steps["row"] for row in range(rows)] for first in firsts]
     tri = pl.pallas_call(
         functools.partial(mix_kernel, places, mine),
         out_shape=jax.ShapeDtypeStruct((devices, 4 * mine, spots // 4), jnp.bfloat16),
@@ -281,12 +282,12 @@
     def update(pair, pair_mask, in_weights, gate_weight, out_weight):
         rows, cols = mesh.shape["row"], mesh.shape["col"]
         if fits(rows, cols, pair, in_weights.shape[1] // 4):
-            plan, col = split_channels, ("y", "x")
-            over = jax.sharding.Mesh(mesh.devices.reshape(rows, 2, 2), ("row", *col))
+            plan, row, col = split_channels, ("z", "core"), ("y", "x")
+            over = jax.sharding.Mesh(mesh.devices.reshape(rows // 2, 2, 2, cols // 2), row + col)
         else:
-            plan, col, over = gather_rows, "col", mesh
-        in_specs = (P("row", col, None), P("row", col), P(), P(), P())
-        out_specs = P("row", col, None)
+            plan, row, col, over = gather_rows, "row", "col", mesh
+        in_specs = (P(row, col, None), P(row, col), P(), P(), P())
+        out_specs = P(row, col, None)
         run = jax.shard_map(plan, mesh=over, in_specs=in_specs, out_specs=out_specs, check_vma=False)
         return run(pair, pair_mask, in_weights, gate_weight, out_weight)
 

time: 31.6 us -> 31.3 us (level)
    all_to_all x1, blocking collectives: 10.5 us -> 9.69 us  [split_channels(): tri = lax.all_to_all(tri, ORDER, 0, 0, tiled=True)]
    all_to_all x1, blocking collectives: 17.5 us -> 18.1 us  [split_channels(): both = lax.all_to_all(both, ORDER, 0, 0, tiled=True)]
where the time goes in v3:
time: 31.3 us; the launch traced here: 31 us
  blocking collectives  27.7 us (88%)
  Pallas kernels  3.23 us (10%)
    all_to_all x1, blocking collectives, split_channels(): both = lax.all_to_all(both, ORDER, 0, 0, tiled=True)  18.1 us
    all_to_all x1, blocking collectives, split_channels(): tri = lax.all_to_all(tri, ORDER, 0, 0, tiled=True)  9.69 us
    pallas_call x1, Pallas kernels, split_channels(): pl.pallas_call(functools.partial(project_kernel, devices, mine, cols_here...  1.58 us
    pallas_call x1, Pallas kernels, split_channels(): pl.pallas_call(finish_kernel, out_shape=jax.ShapeDtypeStruct((spots, widt...  1.03 us

profile of v3, /device:TPU:0, one launch (start us, length us, event | category | flops | bytes accessed | tf_op | source)
XLA Modules:
  0.0 31.0 jit_solution(6309265626983203584)
XLA Ops:
  0.0 1.6 %project.1 = (bf16[32,16,256]{2,1,0:T(8,128)(2,1)S(1)}, bf16[512,128]{1,0:T(8,128)(2,1)S(1)}) custom-call(bf16[512,128]{1,0:T(8,128)(2,1)} %bitcast.2, s32[16,32]{1,0:T(8,128)} %mask_hbm.1, bf16[128,512]{1,0:T(8,128)(2,1)} %weights_hbm.1), custom_call_target="tpu_custom_call" | custom-call | tf_op jit(solution)/shard_map/project/pallas_call | solution.py:236
  1.6 18.1 %all_to_all.10.recv_ref = bf16[32,16,256]{2,1,0:T(8,128)(2,1)S(1)} all-to-all(bf16[32,16,256]{2,1,0:T(8,128)(2,1)S(1)} %get-tuple-element.7), channel_id=1, replica_groups=mesh['z'=4,'core'=2,'y'=2,'x'=2] {'core','x','y','z'}, dimensions={0} | all-to-all | bytes 524288 | tf_op jit(solution)/shard_map/all_to_all | solution.py:252
  19.6 0.6 %mix.1 = bf16[32,16,128]{2,1,0:T(8,128)(2,1)S(1)} custom-call(bf16[32,16,256]{2,1,0:T(8,128)(2,1)S(1)} %all_to_all.10.recv_ref), custom_call_target="tpu_custom_call" | custom-call | tf_op jit(solution)/shard_map/mix/pallas_call | solution.py:253
  20.3 0.0 copy-start
  20.3 0.0 copy-start.1
  20.3 9.7 %all_to_all.11.recv_ref = bf16[32,16,128]{2,1,0:T(8,128)(2,1)S(1)} all-to-all(bf16[32,16,128]{2,1,0:T(8,128)(2,1)S(1)} %mix.1), channel_id=1, replica_groups=mesh['z'=4,'core'=2,'y'=2,'x'=2] {'core','x','y','z'}, dimensions={0} | all-to-all | bytes 262144 | tf_op jit(solution)/shard_map/all_to_all | solution.py:264
  30.0 0.0 copy-done
  30.0 0.0 copy-done.1
  30.0 1.0 %finish.1 = bf16[512,128]{1,0:T(8,128)(2,1)} custom-call(bf16[32,16,128]{2,1,0:T(8,128)(2,1)S(1)} %all_to_all.11.recv_ref, bf16[512,128]{1,0:T(8,128)(2,1)S(1)} %get-tuple-element.8.normed_ref, bf16[128,128]{1,0:T(8,128)(2,1)S(1)} %copy-done, bf16[128,128]{1,0:T(8,128)(2,1)S(1)} %copy-done.1), custom_call_target="tpu_custom_call" | custom-call | tf_op jit(solution)/shard_map/finish/pallas_call | solution.py:265
Async XLA Ops:
  20.3 9.7 %copy-start = (bf16[128,128]{1,0:T(8,128)(2,1)S(1)}, bf16[128,128]{1,0:T(8,128)(2,1)}, u32[]{:S(2)}) copy-start(bf16[128,128]{1,0:T(8,128)(2,1)} %gate_weight_ref.1) | copy-start | bytes 98308
  20.3 9.7 %copy-start.1 = (bf16[128,128]{1,0:T(8,128)(2,1)S(1)}, bf16[128,128]{1,0:T(8,128)(2,1)}, u32[]{:S(2)}) copy-start(bf16[128,128]{1,0:T(8,128)(2,1)} %weight_ref.1) | copy-start | bytes 98308

commit v4 on v3

--- a/solution.py
+++ b/solution.py
@@ -8,7 +8,7 @@
 from jax.experimental.pallas import tpu as pltpu
 from jax.sharding import PartitionSpec as P
 
-ORDER = ("core", "x", "y", "z")
+THERE, BACK = ("x", "y", "z", "core"), ("core", "x", "y", "z")
 
 
 def spread(value, axis, root):
@@ -66,8 +66,9 @@
     hidden = devices * mine
     copies = [(mask_hbm, mask_ref)]
     for source, target in ((weights_hbm, weights_ref), (pair_hbm, pair_ref)):
-        half = source.shape[0] // 2
-        copies += [(source.at[pl.ds(n, half)], target.at[pl.ds(n, half)]) for n in (0, half)]
+        part = source.shape[0] // 4
+        parts = [pl.ds(n * part, part) for n in range(4)]
+        copies += [(source.at[some], target.at[some]) for some in parts]
     copies = [pltpu.make_async_copy(*ends, done.at[n]) for n, ends in enumerate(copies)]
     for copy in copies:
         copy.start()
@@ -127,7 +128,7 @@
 NEAR, FAR, WIDE = 9, 17, 137
 
 
-def mix_kernel(places, mine, recv_ref, send_ref, got, partner, back):
+def mix_kernel(places, back_places, mine, recv_ref, send_ref, got, partner, back):
     rows = len(places[0])
     depth = 4 * mine
     for col, column in enumerate(places):
@@ -176,7 +177,7 @@
             tiles = swap_groups([tri[first : first + 2 * rows] for first in firsts])
             for col, tile in enumerate(tiles):
                 spread_rows(back.at[col], middle * mine + channel, 2 * mine, tile)
-    for col, column in enumerate(places):
+    for col, column in enumerate(back_places):
         for row, place in enumerate(column):
             tiles = [
                 back[col, pl.ds(WIDE * row + NEAR * n, 8, stride=NEAR), :]
@@ -185,9 +186,10 @@
             send_ref[place] = jnp.concatenate(tiles, axis=0).astype(jnp.bfloat16)
 
 
-def finish_kernel(recv_ref, normed_ref, gate_weight_ref, weight_ref, out_hbm, out_ref, done):
+def finish_kernel(owners, recv_ref, normed_ref, gate_weight_ref, weight_ref, out_hbm, out_ref, done):
     devices, depth, width = recv_ref.shape
-    values = recv_ref[...].astype(jnp.float32).reshape(devices // 2, 2, depth // 8, 8, width)
+    values = jnp.stack([recv_ref[place] for place in owners]).astype(jnp.float32)
+    values = values.reshape(devices // 2, 2, depth // 8, 8, width)
     top = lax.broadcasted_iota(jnp.int32, (devices // 2, 8, width), 1) < 4
     weight = weight_ref[...]
     gate = sigmoid(
@@ -216,19 +218,23 @@
     return pltpu.with_memory_space_constraint(values, pltpu.HBM)
 
 
+def places_of(order):
+    sizes = {name: lax.axis_size(name) for name in order}
+    steps = {name: math.prod([sizes[n] for n in order[at + 1 :]]) for at, name in enumerate(order)}
+
+    def offsets(slow, fast):
+        pairs = [(m, n) for m in range(sizes[slow]) for n in range(sizes[fast])]
+        return [m * steps[slow] + n * steps[fast] for m, n in pairs]
+
+    return [[first + row for row in offsets("z", "core")] for first in offsets("y", "x")]
+
+
 def split_channels(pair, pair_mask, in_weights, gate_weight, out_weight):
     rows_here, cols_here, width = pair.shape
     hidden = in_weights.shape[1] // 4
-    sizes = {name: lax.axis_size(name) for name in ORDER}
-    steps = {name: math.prod([sizes[n] for n in ORDER[at + 1 :]]) for at, name in enumerate(ORDER)}
-
-    def offsets(slow, fast):
-        pairs = [(m, n) for m in range(sizes[slow]) for n in range(sizes[fast])]
-        return [m * steps[slow] + n * steps[fast] for m, n in pairs]
-
-    in_rows, in_cols = offsets("z", "core"), offsets("y", "x")
-    places = [[first + row for row in in_rows] for first in in_cols]
-    rows, cols = len(in_rows), len(in_cols)
+    places, back_places = places_of(THERE), places_of(BACK)
+    rows, cols = len(places[0]), len(places)
+    owners = sorted(zip(sum(places, []), sum(back_places, [])))
     devices = rows * cols
     mine = hidden // devices
     spots = rows_here * cols_here
@@ -244,14 +250,14 @@
             pltpu.VMEM((spots, width), pair.dtype),
             pltpu.VMEM(pair_mask.shape, pair_mask.dtype),
             pltpu.VMEM(in_weights.shape, in_weights.dtype),
-            pltpu.SemaphoreType.DMA((5,)),
+            pltpu.SemaphoreType.DMA((9,)),
         ],
         compiler_params=params,
         name="project",
     )(*(in_hbm(values) for values in (pair.reshape(spots, width), pair_mask, in_weights)))
-    both = lax.all_to_all(both, ORDER, 0, 0, tiled=True)
+    both = lax.all_to_all(both, THERE, 0, 0, tiled=True)
     tri = pl.pallas_call(
-        functools.partial(mix_kernel, places, mine),
+        functools.partial(mix_kernel, places, back_places, mine),
         out_shape=jax.ShapeDtypeStruct((devices, 4 * mine, spots // 4), jnp.bfloat16),
         scratch_shapes=[
             pltpu.VMEM((cols, 4, 184, 128), jnp.float32),
@@ -261,9 +267,9 @@
         compiler_params=params,
         name="mix",
     )(both)
-    tri = lax.all_to_all(tri, ORDER, 0, 0, tiled=True)
+    tri = lax.all_to_all(tri, BACK, 0, 0, tiled=True)
     update = pl.pallas_call(
-        finish_kernel,
+        functools.partial(finish_kernel, [place for _, place in owners]),
         out_shape=jax.ShapeDtypeStruct((spots, width), jnp.bfloat16),
         out_specs=pl.BlockSpec(memory_space=pltpu.HBM),
         scratch_shapes=[pltpu.VMEM((spots, width), jnp.bfloat16), pltpu.SemaphoreType.DMA((4,))],

time: 31.3 us -> 31.2 us (level)
  no operation moved by 1% of the time
where the time goes in v4:
time: 31.2 us; the launch traced here: 31 us
  blocking collectives  27.7 us (89%)
  Pallas kernels  3.19 us (10%)
    all_to_all x1, blocking collectives, split_channels(): both = lax.all_to_all(both, THERE, 0, 0, tiled=True)  17.5 us
    all_to_all x1, blocking collectives, split_channels(): tri = lax.all_to_all(tri, BACK, 0, 0, tiled=True)  10.2 us
    pallas_call x1, Pallas kernels, split_channels(): pl.pallas_call(functools.partial(project_kernel, devices, mine, cols_here...  1.54 us
    pallas_call x1, Pallas kernels, split_channels(): pl.pallas_call(functools.partial(finish_kernel, [place for _, place in ow...  1.03 us

profile of v4, /device:TPU:0, one launch (start us, length us, event | category | flops | bytes accessed | tf_op | source)
XLA Modules:
  0.0 31.0 jit_solution(2756699314445942762)
XLA Ops:
  0.0 1.5 %project.1 = (bf16[32,16,256]{2,1,0:T(8,128)(2,1)S(1)}, bf16[512,128]{1,0:T(8,128)(2,1)S(1)}) custom-call(bf16[512,128]{1,0:T(8,128)(2,1)} %bitcast.2, s32[16,32]{1,0:T(8,128)} %mask_hbm.1, bf16[128,512]{1,0:T(8,128)(2,1)} %weights_hbm.1), custom_call_target="tpu_custom_call" | custom-call | tf_op jit(solution)/shard_map/project/pallas_call | solution.py:242
  1.6 17.5 %all_to_all.10.recv_ref = bf16[32,16,256]{2,1,0:T(8,128)(2,1)S(1)} all-to-all(bf16[32,16,256]{2,1,0:T(8,128)(2,1)S(1)} %get-tuple-element.7), channel_id=1, replica_groups=mesh['z'=4,'core'=2,'y'=2,'x'=2] {'x','y','z','core'}, dimensions={0} | all-to-all | bytes 524288 | tf_op jit(solution)/shard_map/all_to_all | solution.py:258
  19.0 0.6 %mix.1 = bf16[32,16,128]{2,1,0:T(8,128)(2,1)S(1)} custom-call(bf16[32,16,256]{2,1,0:T(8,128)(2,1)S(1)} %all_to_all.10.recv_ref), custom_call_target="tpu_custom_call" | custom-call | tf_op jit(solution)/shard_map/mix/pallas_call | solution.py:259
  19.7 0.0 copy-start
  19.7 0.0 copy-start.1
  19.7 10.2 %all_to_all.11.recv_ref = bf16[32,16,128]{2,1,0:T(8,128)(2,1)S(1)} all-to-all(bf16[32,16,128]{2,1,0:T(8,128)(2,1)S(1)} %mix.1), channel_id=1, replica_groups=mesh['z'=4,'core'=2,'y'=2,'x'=2] {'core','x','y','z'}, dimensions={0} | all-to-all | bytes 262144 | tf_op jit(solution)/shard_map/all_to_all | solution.py:270
  29.9 0.0 copy-done
  29.9 0.0 copy-done.1
  29.9 1.0 %finish.1 = bf16[512,128]{1,0:T(8,128)(2,1)} custom-call(bf16[32,16,128]{2,1,0:T(8,128)(2,1)S(1)} %all_to_all.11.recv_ref, bf16[512,128]{1,0:T(8,128)(2,1)S(1)} %get-tuple-element.8.normed_ref, bf16[128,128]{1,0:T(8,128)(2,1)S(1)} %copy-done, bf16[128,128]{1,0:T(8,128)(2,1)S(1)} %copy-done.1), custom_call_target="tpu_custom_call" | custom-call | tf_op jit(solution)/shard_map/finish/pallas_call | solution.py:271
Async XLA Ops:
  19.7 10.3 %copy-start = (bf16[128,128]{1,0:T(8,128)(2,1)S(1)}, bf16[128,128]{1,0:T(8,128)(2,1)}, u32[]{:S(2)}) copy-start(bf16[128,128]{1,0:T(8,128)(2,1)} %gate_weight_ref.1) | copy-start | bytes 98308
  19.7 10.3 %copy-start.1 = (bf16[128,128]{1,0:T(8,128)(2,1)S(1)}, bf16[128,128]{1,0:T(8,128)(2,1)}, u32[]{:S(2)}) copy-start(bf16[128,128]{1,0:T(8,128)(2,1)} %weight_ref.1) | copy-start | bytes 98308

commit v5 on v4

--- a/solution.py
+++ b/solution.py
@@ -200,11 +200,20 @@
         one, two = values[:, 0, n], values[:, 1, n]
         parts.append(jnp.where(top, one, pltpu.roll(two, 4, 1)))
         parts.append(jnp.where(top, pltpu.roll(one, 4, 1), two))
+    parts = [part.reshape(devices * 4, width) for part in parts]
+    stats = []
+    for part in parts:
+        mean = jnp.mean(part, axis=0, keepdims=True)
+        centred = part - mean
+        var = jnp.mean(centred * centred, axis=0, keepdims=True)
+        stats += [mean, jax.lax.rsqrt(var + 1e-05)]
+    stats = jnp.concatenate(stats, axis=0).T
+    total = jnp.sum(weight.astype(jnp.float32), axis=0, keepdims=True)
     copies = []
     for n, part in enumerate(parts):
-        part = layer_norm(part.reshape(devices * 4, width), axis=0)
-        tnorm = part.T.astype(jnp.bfloat16)
-        update = jnp.dot(tnorm, weight, preferred_element_type=jnp.float32)
+        mean, scale = stats[:, 2 * n : 2 * n + 1], stats[:, 2 * n + 1 : 2 * n + 2]
+        update = jnp.dot(part.T.astype(jnp.bfloat16), weight, preferred_element_type=jnp.float32)
+        update = scale * (update - mean * total)
         spots = pl.ds(n * width, width)
         out_ref[spots, :] = (gate[n * width : (n + 1) * width] * update).astype(jnp.bfloat16)
         copies.append(pltpu.make_async_copy(out_ref.at[spots], out_hbm.at[spots], done.at[n]))

time: 31.2 us -> 31.4 us (level)
  no operation moved by 1% of the time
where the time goes in v5:
time: 31.4 us; the launch traced here: 31.1 us
  blocking collectives  27.7 us (88%)
  Pallas kernels  3.34 us (11%)
    all_to_all x1, blocking collectives, split_channels(): both = lax.all_to_all(both, THERE, 0, 0, tiled=True)  17.5 us
    all_to_all x1, blocking collectives, split_channels(): tri = lax.all_to_all(tri, BACK, 0, 0, tiled=True)  10.2 us
    pallas_call x1, Pallas kernels, split_channels(): pl.pallas_call(functools.partial(project_kernel, devices, mine, cols_here...  1.54 us
    pallas_call x1, Pallas kernels, split_channels(): pl.pallas_call(functools.partial(finish_kernel, [place for _, place in ow...  1.17 us

profile of v5, /device:TPU:0, one launch (start us, length us, event | category | flops | bytes accessed | tf_op | source)
XLA Modules:
  0.0 31.1 jit_solution(9403679580073618610)
XLA Ops:
  0.0 1.5 %project.1 = (bf16[32,16,256]{2,1,0:T(8,128)(2,1)S(1)}, bf16[512,128]{1,0:T(8,128)(2,1)S(1)}) custom-call(bf16[512,128]{1,0:T(8,128)(2,1)} %bitcast.2, s32[16,32]{1,0:T(8,128)} %mask_hbm.1, bf16[128,512]{1,0:T(8,128)(2,1)} %weights_hbm.1), custom_call_target="tpu_custom_call" | custom-call | tf_op jit(solution)/shard_map/project/pallas_call | solution.py:251
  1.6 17.5 %all_to_all.10.recv_ref = bf16[32,16,256]{2,1,0:T(8,128)(2,1)S(1)} all-to-all(bf16[32,16,256]{2,1,0:T(8,128)(2,1)S(1)} %get-tuple-element.7), channel_id=1, replica_groups=mesh['z'=4,'core'=2,'y'=2,'x'=2] {'x','y','z','core'}, dimensions={0} | all-to-all | bytes 524288 | tf_op jit(solution)/shard_map/all_to_all | solution.py:267
  19.0 0.6 %mix.1 = bf16[32,16,128]{2,1,0:T(8,128)(2,1)S(1)} custom-call(bf16[32,16,256]{2,1,0:T(8,128)(2,1)S(1)} %all_to_all.10.recv_ref), custom_call_target="tpu_custom_call" | custom-call | tf_op jit(solution)/shard_map/mix/pallas_call | solution.py:268
  19.7 0.0 copy-start
  19.7 0.0 copy-start.1
  19.7 10.2 %all_to_all.11.recv_ref = bf16[32,16,128]{2,1,0:T(8,128)(2,1)S(1)} all-to-all(bf16[32,16,128]{2,1,0:T(8,128)(2,1)S(1)} %mix.1), channel_id=1, replica_groups=mesh['z'=4,'core'=2,'y'=2,'x'=2] {'core','x','y','z'}, dimensions={0} | all-to-all | bytes 262144 | tf_op jit(solution)/shard_map/all_to_all | solution.py:279
  29.9 0.0 copy-done
  29.9 0.0 copy-done.1
  29.9 1.2 %finish.1 = bf16[512,128]{1,0:T(8,128)(2,1)} custom-call(bf16[32,16,128]{2,1,0:T(8,128)(2,1)S(1)} %all_to_all.11.recv_ref, bf16[512,128]{1,0:T(8,128)(2,1)S(1)} %get-tuple-element.8.normed_ref, bf16[128,128]{1,0:T(8,128)(2,1)S(1)} %copy-done, bf16[128,128]{1,0:T(8,128)(2,1)S(1)} %copy-done.1), custom_call_target="tpu_custom_call" | custom-call | tf_op jit(solution)/shard_map/finish/pallas_call | solution.py:280
Async XLA Ops:
  19.7 10.3 %copy-start = (bf16[128,128]{1,0:T(8,128)(2,1)S(1)}, bf16[128,128]{1,0:T(8,128)(2,1)}, u32[]{:S(2)}) copy-start(bf16[128,128]{1,0:T(8,128)(2,1)} %gate_weight_ref.1) | copy-start | bytes 98308
  19.7 10.3 %copy-start.1 = (bf16[128,128]{1,0:T(8,128)(2,1)S(1)}, bf16[128,128]{1,0:T(8,128)(2,1)}, u32[]{:S(2)}) copy-start(bf16[128,128]{1,0:T(8,128)(2,1)} %weight_ref.1) | copy-start | bytes 98308

commit v6 on v3

--- a/solution.py
+++ b/solution.py
@@ -66,8 +66,9 @@
     hidden = devices * mine
     copies = [(mask_hbm, mask_ref)]
     for source, target in ((weights_hbm, weights_ref), (pair_hbm, pair_ref)):
-        half = source.shape[0] // 2
-        copies += [(source.at[pl.ds(n, half)], target.at[pl.ds(n, half)]) for n in (0, half)]
+        part = source.shape[0] // 4
+        parts = [pl.ds(n * part, part) for n in range(4)]
+        copies += [(source.at[some], target.at[some]) for some in parts]
     copies = [pltpu.make_async_copy(*ends, done.at[n]) for n, ends in enumerate(copies)]
     for copy in copies:
         copy.start()
@@ -85,16 +86,18 @@
         copy.wait()
     weights = weights_ref[...]
 
-    def in_order(block):
-        both = [weights[:, (block + n) * hidden : (block + n + 1) * hidden] for n in (0, 2)]
-        return dot_t(order, jnp.concatenate(both, axis=1)).astype(jnp.bfloat16)
+    blocks = [weights[:, n * hidden : (n + 1) * hidden] for n in range(4)]
+    pairs = [jnp.concatenate(blocks[n::2], axis=1) for n in range(2)]
+    ordered = dot_t(order, jnp.concatenate(pairs, axis=0)).astype(jnp.bfloat16)
+    ordered = jnp.concatenate([ordered[:, :width], ordered[:, width:]], axis=0)
 
     mask = mask_ref[...].astype(jnp.float32).astype(jnp.bfloat16)
     mask = jnp.dot(mask, spread_cols, preferred_element_type=jnp.float32)
     mask = jnp.sum(jnp.where(own, mask, 0.0), axis=0, keepdims=True)
     normed = layer_norm(pair_ref[...].astype(jnp.float32)).astype(jnp.bfloat16)
     normed_ref[...] = normed
-    both = mask * sigmoid(dot_t(in_order(1), normed)) * dot_t(in_order(0), normed)
+    proj = dot_t(ordered, normed)
+    both = mask * sigmoid(proj[2 * hidden :]) * proj[: 2 * hidden]
     both = both.reshape(devices, 2 * mine, spots)
     half = spots // 2
     both = jnp.concatenate([both[:, :, :half], both[:, :, half:]], axis=1)
@@ -198,13 +201,13 @@
         one, two = values[:, 0, n], values[:, 1, n]
         parts.append(jnp.where(top, one, pltpu.roll(two, 4, 1)))
         parts.append(jnp.where(top, pltpu.roll(one, 4, 1), two))
+    parts = [layer_norm(part.reshape(devices * 4, width), axis=0).T for part in parts]
+    tnorm = jnp.concatenate(parts, axis=0).astype(jnp.bfloat16)
+    update = jnp.dot(tnorm, weight, preferred_element_type=jnp.float32)
+    out_ref[...] = (gate * update).astype(jnp.bfloat16)
     copies = []
-    for n, part in enumerate(parts):
-        part = layer_norm(part.reshape(devices * 4, width), axis=0)
-        tnorm = part.T.astype(jnp.bfloat16)
-        update = jnp.dot(tnorm, weight, preferred_element_type=jnp.float32)
+    for n in range(len(parts)):
         spots = pl.ds(n * width, width)
-        out_ref[spots, :] = (gate[n * width : (n + 1) * width] * update).astype(jnp.bfloat16)
         copies.append(pltpu.make_async_copy(out_ref.at[spots], out_hbm.at[spots], done.at[n]))
     for copy in copies:
         copy.start()
@@ -244,7 +247,7 @@
             pltpu.VMEM((spots, width), pair.dtype),
             pltpu.VMEM(pair_mask.shape, pair_mask.dtype),
             pltpu.VMEM(in_weights.shape, in_weights.dtype),
-            pltpu.SemaphoreType.DMA((5,)),
+            pltpu.SemaphoreType.DMA((9,)),
         ],
         compiler_params=params,
         name="project",

time: 31.3 us -> 31.2 us (level)
  no operation moved by 1% of the time
where the time goes in v6:
time: 31.2 us; the launch traced here: 30.9 us
  blocking collectives  27.7 us (89%)
  Pallas kernels  3.15 us (10%)
    all_to_all x1, blocking collectives, split_channels(): both = lax.all_to_all(both, ORDER, 0, 0, tiled=True)  18.1 us
    all_to_all x1, blocking collectives, split_channels(): tri = lax.all_to_all(tri, ORDER, 0, 0, tiled=True)  9.69 us
    pallas_call x1, Pallas kernels, split_channels(): pl.pallas_call(functools.partial(project_kernel, devices, mine, cols_here...  1.5 us
    pallas_call x1, Pallas kernels, split_channels(): pl.pallas_call(finish_kernel, out_shape=jax.ShapeDtypeStruct((spots, widt...  1.03 us

profile of v6, /device:TPU:0, one launch (start us, length us, event | category | flops | bytes accessed | tf_op | source)
XLA Modules:
  0.0 30.9 jit_solution(639008578141623243)
XLA Ops:
  0.0 1.5 %project.1 = (bf16[32,16,256]{2,1,0:T(8,128)(2,1)S(1)}, bf16[512,128]{1,0:T(8,128)(2,1)S(1)}) custom-call(bf16[512,128]{1,0:T(8,128)(2,1)} %bitcast.2, s32[16,32]{1,0:T(8,128)} %mask_hbm.1, bf16[128,512]{1,0:T(8,128)(2,1)} %weights_hbm.1), custom_call_target="tpu_custom_call" | custom-call | tf_op jit(solution)/shard_map/project/pallas_call | solution.py:239
  1.5 18.1 %all_to_all.10.recv_ref = bf16[32,16,256]{2,1,0:T(8,128)(2,1)S(1)} all-to-all(bf16[32,16,256]{2,1,0:T(8,128)(2,1)S(1)} %get-tuple-element.7), channel_id=1, replica_groups=mesh['z'=4,'core'=2,'y'=2,'x'=2] {'core','x','y','z'}, dimensions={0} | all-to-all | bytes 524288 | tf_op jit(solution)/shard_map/all_to_all | solution.py:255
  19.6 0.6 %mix.1 = bf16[32,16,128]{2,1,0:T(8,128)(2,1)S(1)} custom-call(bf16[32,16,256]{2,1,0:T(8,128)(2,1)S(1)} %all_to_all.10.recv_ref), custom_call_target="tpu_custom_call" | custom-call | tf_op jit(solution)/shard_map/mix/pallas_call | solution.py:256
  20.2 0.0 copy-start
  20.2 0.0 copy-start.1
  20.2 9.7 %all_to_all.11.recv_ref = bf16[32,16,128]{2,1,0:T(8,128)(2,1)S(1)} all-to-all(bf16[32,16,128]{2,1,0:T(8,128)(2,1)S(1)} %mix.1), channel_id=1, replica_groups=mesh['z'=4,'core'=2,'y'=2,'x'=2] {'core','x','y','z'}, dimensions={0} | all-to-all | bytes 262144 | tf_op jit(solution)/shard_map/all_to_all | solution.py:267
  29.9 0.0 copy-done
  29.9 0.0 copy-done.1
  29.9 1.0 %finish.1 = bf16[512,128]{1,0:T(8,128)(2,1)} custom-call(bf16[32,16,128]{2,1,0:T(8,128)(2,1)S(1)} %all_to_all.11.recv_ref, bf16[512,128]{1,0:T(8,128)(2,1)S(1)} %get-tuple-element.8.normed_ref, bf16[128,128]{1,0:T(8,128)(2,1)S(1)} %copy-done, bf16[128,128]{1,0:T(8,128)(2,1)S(1)} %copy-done.1), custom_call_target="tpu_custom_call" | custom-call | tf_op jit(solution)/shard_map/finish/pallas_call | solution.py:268
Async XLA Ops:
  20.2 9.7 %copy-start = (bf16[128,128]{1,0:T(8,128)(2,1)S(1)}, bf16[128,128]{1,0:T(8,128)(2,1)}, u32[]{:S(2)}) copy-start(bf16[128,128]{1,0:T(8,128)(2,1)} %gate_weight_ref.1) | copy-start | bytes 98308
  20.2 9.7 %copy-start.1 = (bf16[128,128]{1,0:T(8,128)(2,1)S(1)}, bf16[128,128]{1,0:T(8,128)(2,1)}, u32[]{:S(2)}) copy-start(bf16[128,128]{1,0:T(8,128)(2,1)} %weight_ref.1) | copy-start | bytes 98308

commit v7 on v6

--- a/solution.py
+++ b/solution.py
@@ -70,8 +70,8 @@
         parts = [pl.ds(n * part, part) for n in range(4)]
         copies += [(source.at[some], target.at[some]) for some in parts]
     copies = [pltpu.make_async_copy(*ends, done.at[n]) for n, ends in enumerate(copies)]
-    for copy in copies:
-        copy.start()
+    for n, copy in enumerate(copies):
+        copy.start(priority=n % 2)
     shape = (2 * hidden, 2 * hidden)
     row, col = (lax.broadcasted_iota(jnp.int32, shape, n) for n in (0, 1))
     source = (row // mine) % 2 * hidden + row // (2 * mine) * mine + row % mine
@@ -209,8 +209,8 @@
     for n in range(len(parts)):
         spots = pl.ds(n * width, width)
         copies.append(pltpu.make_async_copy(out_ref.at[spots], out_hbm.at[spots], done.at[n]))
-    for copy in copies:
-        copy.start()
+    for n, copy in enumerate(copies):
+        copy.start(priority=n % 2)
     for copy in copies:
         copy.wait()
 

time: 31.2 us -> 31.2 us (level)
  no operation moved by 1% of the time
where the time goes in v7:
time: 31.2 us; the launch traced here: 30.9 us
  blocking collectives  27.7 us (89%)
  Pallas kernels  3.15 us (10%)
    all_to_all x1, blocking collectives, split_channels(): both = lax.all_to_all(both, ORDER, 0, 0, tiled=True)  18.1 us
    all_to_all x1, blocking collectives, split_channels(): tri = lax.all_to_all(tri, ORDER, 0, 0, tiled=True)  9.69 us
    pallas_call x1, Pallas kernels, split_channels(): pl.pallas_call(functools.partial(project_kernel, devices, mine, cols_here...  1.5 us
    pallas_call x1, Pallas kernels, split_channels(): pl.pallas_call(finish_kernel, out_shape=jax.ShapeDtypeStruct((spots, widt...  1.03 us

profile of v7, /device:TPU:0, one launch (start us, length us, event | category | flops | bytes accessed | tf_op | source)
XLA Modules:
  0.0 30.9 jit_solution(2113607000038079976)
XLA Ops:
  0.0 1.5 %project.1 = (bf16[32,16,256]{2,1,0:T(8,128)(2,1)S(1)}, bf16[512,128]{1,0:T(8,128)(2,1)S(1)}) custom-call(bf16[512,128]{1,0:T(8,128)(2,1)} %bitcast.2, s32[16,32]{1,0:T(8,128)} %mask_hbm.1, bf16[128,512]{1,0:T(8,128)(2,1)} %weights_hbm.1), custom_call_target="tpu_custom_call" | custom-call | tf_op jit(solution)/shard_map/project/pallas_call | solution.py:239
  1.5 18.1 %all_to_all.10.recv_ref = bf16[32,16,256]{2,1,0:T(8,128)(2,1)S(1)} all-to-all(bf16[32,16,256]{2,1,0:T(8,128)(2,1)S(1)} %get-tuple-element.7), channel_id=1, replica_groups=mesh['z'=4,'core'=2,'y'=2,'x'=2] {'core','x','y','z'}, dimensions={0} | all-to-all | bytes 524288 | tf_op jit(solution)/shard_map/all_to_all | solution.py:255
  19.6 0.6 %mix.1 = bf16[32,16,128]{2,1,0:T(8,128)(2,1)S(1)} custom-call(bf16[32,16,256]{2,1,0:T(8,128)(2,1)S(1)} %all_to_all.10.recv_ref), custom_call_target="tpu_custom_call" | custom-call | tf_op jit(solution)/shard_map/mix/pallas_call | solution.py:256
  20.2 0.0 copy-start
  20.2 0.0 copy-start.1
  20.2 9.7 %all_to_all.11.recv_ref = bf16[32,16,128]{2,1,0:T(8,128)(2,1)S(1)} all-to-all(bf16[32,16,128]{2,1,0:T(8,128)(2,1)S(1)} %mix.1), channel_id=1, replica_groups=mesh['z'=4,'core'=2,'y'=2,'x'=2] {'core','x','y','z'}, dimensions={0} | all-to-all | bytes 262144 | tf_op jit(solution)/shard_map/all_to_all | solution.py:267
  29.9 0.0 copy-done
  29.9 0.0 copy-done.1
  29.9 1.0 %finish.1 = bf16[512,128]{1,0:T(8,128)(2,1)} custom-call(bf16[32,16,128]{2,1,0:T(8,128)(2,1)S(1)} %all_to_all.11.recv_ref, bf16[512,128]{1,0:T(8,128)(2,1)S(1)} %get-tuple-element.8.normed_ref, bf16[128,128]{1,0:T(8,128)(2,1)S(1)} %copy-done, bf16[128,128]{1,0:T(8,128)(2,1)S(1)} %copy-done.1), custom_call_target="tpu_custom_call" | custom-call | tf_op jit(solution)/shard_map/finish/pallas_call | solution.py:268
Async XLA Ops:
  20.2 9.7 %copy-start = (bf16[128,128]{1,0:T(8,128)(2,1)S(1)}, bf16[128,128]{1,0:T(8,128)(2,1)}, u32[]{:S(2)}) copy-start(bf16[128,128]{1,0:T(8,128)(2,1)} %gate_weight_ref.1) | copy-start | bytes 98308
  20.2 9.7 %copy-start.1 = (bf16[128,128]{1,0:T(8,128)(2,1)S(1)}, bf16[128,128]{1,0:T(8,128)(2,1)}, u32[]{:S(2)}) copy-start(bf16[128,128]{1,0:T(8,128)(2,1)} %weight_ref.1) | copy-start | bytes 98308
